TPU v7x, 32 devices: a whole 2x2x4 slice. The times are simulated.
32 devices in a mesh: lon: 8 (over z, y), bin: 4 (over x, core).
Axes of the slice: x: 2, y: 2, z: 4, core: 2. Of those that a mesh axis runs over, the one named last changes fastest.
Arguments:
- adjoint_start: float32 [8, 4, 8, 1024], P('bin', None, None, 'lon'), may hold values from -6 to 6
- base_flux: float32 [8, 8, 1024], P('bin', None, 'lon'), may hold values from 0.1 to 1
- vertical_mixing: float32 [3, 8, 1024], P(None, None, 'lon'), may hold values from 0.05 to 5
- zonal_fraction: float32 [4, 8], replicated, may hold values from 0.02 to 0.98
- meridional_fraction: float32 [4], replicated, may hold values from 0.05 to 0.95
- zonal_hops: int32 [8], replicated, may hold values from -3 to 3, as said below
- cell_shift: int32 [8], replicated, may hold values from 0 to 127, as said below
Outputs:
- adjoint_end: float32 [8, 4, 8, 1024], P('bin', None, None, 'lon')
- emission_gradient: float32 [8, 1024], P(None, 'lon')
Inputs may be any that keep to these rules, and one draw needn't show every extreme that they name: For every h from 1 to 3, exactly (3 - h + 1) * 1 rows have zonal_hops >= h and exactly as many have zonal_hops <= -h. `cell_shift`: both extreme values occur.
All inputs are finite; a program needn't handle non-finite values.
Results may differ from a plain program's by a relative error of at most 0.0001.
Values sent between devices are 32-bit elements; how exact they have to be, the bound alone decides.
A program may use at most 64 MiB of HBM per device.

v0:
```python
import jax
import jax.numpy as jnp
from jax import lax
from jax.sharding import PartitionSpec as P

HMAX = 3
STEPS = 2
right_face = (0.0, -1.0, 7.0, 7.0, -1.0)
slope_face = (1.0, -8.0, 0.0, 8.0, -1.0)
curve_face = (3.0, -18.0, 30.0, -18.0, 3.0)


def padded_2(block, sides, width):
    for axis, dim in sides:
        count = lax.axis_size(axis)
        forward = [(i, i + 1) for i in range(count - 1)]
        forward.append((count - 1, 0))
        backward = [(target, source) for source, target in forward]
        low = lax.ppermute(
            lax.slice_in_dim(block, block.shape[dim] - width, None, axis=dim), axis, forward
        )
        high = lax.ppermute(lax.slice_in_dim(block, 0, width, axis=dim), axis, backward)
        block = jnp.concatenate([low, block, high], axis=dim)
    return block


def from_behind(value, axis, by):
    length = lax.axis_size(axis)
    return lax.ppermute(value, axis, [(i, (i + by) % length) for i in range(length)])


def flux_weights(courant):
    square = courant * courant
    cubic_part = 0.5 * square * (1.0 - courant * (2.0 / 3.0))
    return [
        (
            courant * right_face[offset]
            - 0.5 * square * slope_face[offset]
            + cubic_part * curve_face[offset]
        )
        / 12.0
        for offset in range(5)
    ]


def vertical_solve(adjoint_field, vertical_mixing):
    levels = adjoint_field.shape[1]
    ratios = []
    values = []
    for layer_index in range(levels):
        pivot_value = 1.0
        source_row = adjoint_field[:, layer_index]
        if layer_index < levels - 1:
            pivot_value = pivot_value + vertical_mixing[layer_index]
        if layer_index > 0:
            below = vertical_mixing[layer_index - 1]
            pivot_value = pivot_value + below + below * ratios[-1]
            source_row = source_row + below * values[-1]
        values.append(source_row / pivot_value)
        if layer_index < levels - 1:
            ratios.append(-vertical_mixing[layer_index] / pivot_value)
    solved = [values[levels - 1]]
    for layer_index in range(levels - 2, -1, -1):
        solved.insert(0, values[layer_index] - ratios[layer_index] * solved[0])
    return jnp.stack(solved, axis=1)


def zonal_adjoint(adjoint_field, zonal_fraction):
    sector_width = adjoint_field.shape[3]
    weights = flux_weights(zonal_fraction)
    padded = padded_2(adjoint_field, (("lon", 3),), 3)
    face_flux = 0.0
    for offset in range(5):
        start_col = 3 - (offset - 2)
        face_flux = (
            face_flux
            + weights[offset][:, :, None]
            * padded[:, :, :, start_col : start_col + sector_width + 1]
        )
    return adjoint_field - face_flux[:, :, :, :sector_width] + face_flux[:, :, :, 1:]


def roll_rows(field_data, offsets):
    width = field_data.shape[3]
    bit_count = max(1, (width - 1).bit_length())
    for bit_index in range(bit_count):
        amount = 1 << bit_index
        moved = jnp.roll(field_data, -amount, axis=3)
        chosen = (offsets // amount % 2)[None, None, :, None] == 1
        field_data = jnp.where(chosen, moved, field_data)
    return field_data


def pick_cells(adjoint_field, following, cell_shift):
    sector_width = adjoint_field.shape[3]
    joined = jnp.concatenate([adjoint_field, following], axis=3)
    return roll_rows(joined, cell_shift)[:, :, :, :sector_width]


def hop_shift(adjoint_field, zonal_hops, cell_shift):
    following = from_behind(adjoint_field, "lon", -1)
    picked = pick_cells(adjoint_field, following, cell_shift)
    hop_rows = zonal_hops[None, None, :, None]
    eastern = jnp.where(hop_rows > 0, picked, 0.0)
    western = jnp.where(hop_rows < 0, picked, 0.0)
    result_field = jnp.where(hop_rows == 0, picked, 0.0)
    for hop_count in range(1, HMAX + 1):
        eastern = from_behind(eastern, "lon", -1)
        western = from_behind(western, "lon", 1)
        result_field = result_field + jnp.where(hop_rows == hop_count, eastern, 0.0)
        result_field = result_field + jnp.where(hop_rows == -hop_count, western, 0.0)
    return result_field


def meridional_adjoint(adjoint_field, meridional_fraction):
    lat_count = adjoint_field.shape[2]
    weights = flux_weights(meridional_fraction)
    padded = jnp.pad(adjoint_field, ((0, 0), (0, 0), (3, 3), (0, 0)))
    face_flux = 0.0
    for offset in range(5):
        start_row = 3 - (offset - 2)
        face_flux = (
            face_flux
            + weights[offset][:, None, None] * padded[:, :, start_row : start_row + lat_count + 1]
        )
    return adjoint_field - face_flux[:, :, :lat_count] + face_flux[:, :, 1:]


def per_device(
    adjoint_start,
    base_flux,
    vertical_mixing,
    zonal_fraction,
    meridional_fraction,
    zonal_hops,
    cell_shift,
):
    adjoint_field = adjoint_start
    gradient_sum = jnp.zeros(base_flux.shape[1:], jnp.float32)
    for step_index in range(STEPS):
        adjoint_field = vertical_solve(adjoint_field, vertical_mixing)
        adjoint_field = zonal_adjoint(adjoint_field, zonal_fraction)
        adjoint_field = hop_shift(adjoint_field, zonal_hops, cell_shift)
        adjoint_field = meridional_adjoint(adjoint_field, meridional_fraction)
        local_term = jnp.sum(base_flux * adjoint_field[:, 0], axis=0)
        gradient_sum = gradient_sum + lax.psum(local_term, "bin")
    return (adjoint_field, gradient_sum)


def solution(mesh):
    return jax.shard_map(
        per_device,
        mesh=mesh,
        in_specs=(
            P("bin", None, None, "lon"),
            P("bin", None, "lon"),
            P(None, None, "lon"),
            P(),
            P(),
            P(),
            P(),
        ),
        out_specs=(P("bin", None, None, "lon"), P(None, "lon")),
        check_vma=False,
    )
```

profile of v0, /device:TPU:0, one launch (start us, length us, event | category | flops | bytes accessed | tf_op | source)
XLA Modules:
  0.0 83.2 jit_solution(6797585602489341325)
XLA Ops:
  0.6 0.8 fusion.54
  1.4 0.7 copy-done.2
  2.3 6.0 %collective-permute-start = (f32[2,4,8,3]{3,2,1,0:T(8,128)S(1)}, f32[2,4,8,3]{3,2,1,0:T(8,128)S(1)}, u32[]{:S(2)}, u32[]{:S(2)}) collective-permute-start(f32[2,4,8,3]{3,2,1,0:T(8,128)S(1)} %get-tuple-element.30), channel_id=1, source_target_pairs={{4,0},{8,4},{12,8},{16,12},{20,16},{24,20},{28,24},{0,28},{5,1},{9... | collective-permute-start | bytes 2312 | tf_op jit(solution)/shard_map/ppermute | solution.py:22
  8.3 0.6 copy-done.5
  9.0 0.9 %collective-permute-done = f32[2,4,8,3]{3,2,1,0:T(8,128)S(1)} collective-permute-done((f32[2,4,8,3]{3,2,1,0:T(8,128)S(1)}, f32[2,4,8,3]{3,2,1,0:T(8,128)S(1)}, u32[]{:S(2)}, u32[]{:S(2)}) %collective-permute-start) | collective-permute-done | bytes 800 | tf_op jit(solution)/shard_map/ppermute | solution.py:22
  9.9 5.0 %collective-permute-done.1 = f32[2,4,8,3]{3,2,1,0:T(8,128)S(1)} collective-permute-done((f32[2,4,8,3]{3,2,1,0:T(8,128)S(1)}, f32[2,4,8,3]{3,2,1,0:T(8,128)S(1)}, u32[]{:S(2)}, u32[]{:S(2)}) %collective-permute-start.1) | collective-permute-done | bytes 800 | tf_op jit(solution)/shard_map/ppermute | solution.py:19
  14.9 0.1 pad_maximum_fusion.2
  15.0 0.2 fusion.26
  15.2 0.1 slice_add_fusion.3
  15.3 0.6 copy-done.6
  15.9 3.3 %collective-permute-done.2 = f32[2,4,8,128]{3,2,1,0:T(8,128)S(1)} collective-permute-done((f32[2,4,8,128]{3,2,1,0:T(8,128)S(1)}, f32[2,4,8,128]{3,2,1,0:T(8,128)S(1)}, u32[]{:S(2)}, u32[]{:S(2)}) %collective-permute-start.2) | collective-permute-done | bytes 32800 | tf_op jit(solution)/shard_map/ppermute | solution.py:29
  19.2 0.1 fusion.2
  19.3 0.1 fusion.3
  19.4 0.1 slice.368
  19.5 0.1 maximum_select_fusion
  19.5 0.1 slice.370
  19.6 0.1 maximum_select_fusion.1
  19.7 0.1 slice.372
  19.8 0.1 maximum_select_fusion.2
  19.9 0.1 slice.374
  20.0 0.1 maximum_select_fusion.3
  20.1 0.1 slice.376
  20.2 0.1 maximum_select_fusion.4
  20.3 0.1 slice.378
  20.4 0.1 maximum_select_fusion.5
  20.5 0.1 broadcast_select_fusion.2
  20.6 4.7 %collective-permute-start.3 = (f32[2,4,8,128]{3,2,1,0:T(8,128)S(1)}, f32[2,4,8,128]{3,2,1,0:T(8,128)S(1)}, u32[]{:S(2)}, u32[]{:S(2)}) collective-permute-start(f32[2,4,8,128]{3,2,1,0:T(8,128)S(1)} %get-tuple-element.10), channel_id=1, source_target_pairs={{0,28},{4,0},{8,4},{12,8},{16,12},{20,16},{24,20},{28,24},{1,29},{... | collective-permute-start | bytes 98312 | tf_op jit(solution)/shard_map/ppermute | solution.py:29
  25.4 1.9 %collective-permute-done.4 = f32[2,4,8,128]{3,2,1,0:T(8,128)S(1)} collective-permute-done((f32[2,4,8,128]{3,2,1,0:T(8,128)S(1)}, f32[2,4,8,128]{3,2,1,0:T(8,128)S(1)}, u32[]{:S(2)}, u32[]{:S(2)}) %collective-permute-start.4) | collective-permute-done | bytes 32800 | tf_op jit(solution)/shard_map/ppermute | solution.py:29
  27.2 4.8 %collective-permute-start.5 = (f32[2,4,8,128]{3,2,1,0:T(8,128)S(1)}, f32[2,4,8,128]{3,2,1,0:T(8,128)S(1)}, u32[]{:S(2)}, u32[]{:S(2)}) collective-permute-start(f32[2,4,8,128]{3,2,1,0:T(8,128)S(1)} %collective-permute-done.3), channel_id=1, source_target_pairs={{0,28},{4,0},{8,4},{12,8},{16,12},{20,16},{24,20},{28,24},{1,29},{... | collective-permute-start | bytes 98312 | tf_op jit(solution)/shard_map/ppermute | solution.py:29
  32.1 1.8 %collective-permute-done.6 = f32[2,4,8,128]{3,2,1,0:T(8,128)S(1)} collective-permute-done((f32[2,4,8,128]{3,2,1,0:T(8,128)S(1)}, f32[2,4,8,128]{3,2,1,0:T(8,128)S(1)}, u32[]{:S(2)}, u32[]{:S(2)}) %collective-permute-start.6) | collective-permute-done | bytes 32800 | tf_op jit(solution)/shard_map/ppermute | solution.py:29
  33.9 5.0 %collective-permute-start.7 = (f32[2,4,8,128]{3,2,1,0:T(8,128)S(1)}, f32[2,4,8,128]{3,2,1,0:T(8,128)S(1)}, u32[]{:S(2)}, u32[]{:S(2)}) collective-permute-start(f32[2,4,8,128]{3,2,1,0:T(8,128)S(1)} %collective-permute-done.5), channel_id=1, source_target_pairs={{0,28},{4,0},{8,4},{12,8},{16,12},{20,16},{24,20},{28,24},{1,29},{... | collective-permute-start | bytes 98312 | tf_op jit(solution)/shard_map/ppermute | solution.py:29
  38.8 2.0 %collective-permute-done.8 = f32[2,4,8,128]{3,2,1,0:T(8,128)S(1)} collective-permute-done((f32[2,4,8,128]{3,2,1,0:T(8,128)S(1)}, f32[2,4,8,128]{3,2,1,0:T(8,128)S(1)}, u32[]{:S(2)}, u32[]{:S(2)}) %collective-permute-start.8) | collective-permute-done | bytes 32800 | tf_op jit(solution)/shard_map/ppermute | solution.py:29
  40.8 0.1 select_add_fusion.1
  40.9 0.1 fusion.8
  41.1 4.7 %collective-permute-start.9 = (f32[2,4,8,3]{3,2,1,0:T(8,128)S(1)}, f32[2,4,8,3]{3,2,1,0:T(8,128)S(1)}, u32[]{:S(2)}, u32[]{:S(2)}) collective-permute-start(f32[2,4,8,3]{3,2,1,0:T(8,128)S(1)} %get-tuple-element.26), channel_id=1, source_target_pairs={{4,0},{8,4},{12,8},{16,12},{20,16},{24,20},{28,24},{0,28},{5,1},{9... | collective-permute-start | bytes 2312 | tf_op jit(solution)/shard_map/ppermute | solution.py:22
  45.9 1.9 %collective-permute-done.10 = f32[2,4,8,3]{3,2,1,0:T(8,128)S(1)} collective-permute-done((f32[2,4,8,3]{3,2,1,0:T(8,128)S(1)}, f32[2,4,8,3]{3,2,1,0:T(8,128)S(1)}, u32[]{:S(2)}, u32[]{:S(2)}) %collective-permute-start.10) | collective-permute-done | bytes 800 | tf_op jit(solution)/shard_map/ppermute | solution.py:19
  47.8 0.1 pad_maximum_fusion.3
  47.8 0.2 fusion.22
  48.0 0.1 slice_add_fusion.1
  48.1 4.7 %collective-permute-start.11 = (f32[2,4,8,128]{3,2,1,0:T(8,128)S(1)}, f32[2,4,8,128]{3,2,1,0:T(8,128)S(1)}, u32[]{:S(2)}, u32[]{:S(2)}) collective-permute-start(f32[2,4,8,128]{3,2,1,0:T(8,128)S(1)} %slice_add_fusion.1), channel_id=1, source_target_pairs={{0,28},{4,0},{8,4},{12,8},{16,12},{20,16},{24,20},{28,24},{1,29},{... | collective-permute-start | bytes 98312 | tf_op jit(solution)/shard_map/ppermute | solution.py:29
  52.8 1.6 %collective-permute-done.11 = f32[2,4,8,128]{3,2,1,0:T(8,128)S(1)} collective-permute-done((f32[2,4,8,128]{3,2,1,0:T(8,128)S(1)}, f32[2,4,8,128]{3,2,1,0:T(8,128)S(1)}, u32[]{:S(2)}, u32[]{:S(2)}) %collective-permute-start.11) | collective-permute-done | bytes 32800 | tf_op jit(solution)/shard_map/ppermute | solution.py:29
  54.4 0.1 fusion
  54.5 0.1 fusion.1
  54.6 0.1 slice.401
  54.7 0.1 maximum_select_fusion.6
  54.8 0.1 slice.403
  54.9 0.1 maximum_select_fusion.7
  55.0 0.1 slice.405
  55.0 0.1 maximum_select_fusion.8
  55.1 0.1 slice.407
  55.2 0.1 maximum_select_fusion.9
  55.4 0.1 maximum_select_fusion.10
  55.6 0.1 maximum_select_fusion.11
  55.7 0.1 broadcast_select_fusion.3
  55.9 5.1 %collective-permute-start.12 = (f32[2,4,8,128]{3,2,1,0:T(8,128)S(1)}, f32[2,4,8,128]{3,2,1,0:T(8,128)S(1)}, u32[]{:S(2)}, u32[]{:S(2)}) collective-permute-start(f32[2,4,8,128]{3,2,1,0:T(8,128)S(1)} %get-tuple-element.4), channel_id=1, source_target_pairs={{0,28},{4,0},{8,4},{12,8},{16,12},{20,16},{24,20},{28,24},{1,29},{... | collective-permute-start | bytes 98312 | tf_op jit(solution)/shard_map/ppermute | solution.py:29
  60.9 1.8 %collective-permute-done.13 = f32[2,4,8,128]{3,2,1,0:T(8,128)S(1)} collective-permute-done((f32[2,4,8,128]{3,2,1,0:T(8,128)S(1)}, f32[2,4,8,128]{3,2,1,0:T(8,128)S(1)}, u32[]{:S(2)}, u32[]{:S(2)}) %collective-permute-start.13) | collective-permute-done | bytes 32800 | tf_op jit(solution)/shard_map/ppermute | solution.py:29
  62.8 4.8 %collective-permute-start.14 = (f32[2,4,8,128]{3,2,1,0:T(8,128)S(1)}, f32[2,4,8,128]{3,2,1,0:T(8,128)S(1)}, u32[]{:S(2)}, u32[]{:S(2)}) collective-permute-start(f32[2,4,8,128]{3,2,1,0:T(8,128)S(1)} %collective-permute-done.12), channel_id=1, source_target_pairs={{0,28},{4,0},{8,4},{12,8},{16,12},{20,16},{24,20},{28,24},{1,29},{... | collective-permute-start | bytes 98312 | tf_op jit(solution)/shard_map/ppermute | solution.py:29
  67.5 1.8 %collective-permute-done.15 = f32[2,4,8,128]{3,2,1,0:T(8,128)S(1)} collective-permute-done((f32[2,4,8,128]{3,2,1,0:T(8,128)S(1)}, f32[2,4,8,128]{3,2,1,0:T(8,128)S(1)}, u32[]{:S(2)}, u32[]{:S(2)}) %collective-permute-start.15) | collective-permute-done | bytes 32800 | tf_op jit(solution)/shard_map/ppermute | solution.py:29
  69.4 4.8 %collective-permute-start.16 = (f32[2,4,8,128]{3,2,1,0:T(8,128)S(1)}, f32[2,4,8,128]{3,2,1,0:T(8,128)S(1)}, u32[]{:S(2)}, u32[]{:S(2)}) collective-permute-start(f32[2,4,8,128]{3,2,1,0:T(8,128)S(1)} %collective-permute-done.14), channel_id=1, source_target_pairs={{0,28},{4,0},{8,4},{12,8},{16,12},{20,16},{24,20},{28,24},{1,29},{... | collective-permute-start | bytes 98312 | tf_op jit(solution)/shard_map/ppermute | solution.py:29
  74.2 1.8 %collective-permute-done.17 = f32[2,4,8,128]{3,2,1,0:T(8,128)S(1)} collective-permute-done((f32[2,4,8,128]{3,2,1,0:T(8,128)S(1)}, f32[2,4,8,128]{3,2,1,0:T(8,128)S(1)}, u32[]{:S(2)}, u32[]{:S(2)}) %collective-permute-start.17) | collective-permute-done | bytes 32800 | tf_op jit(solution)/shard_map/ppermute | solution.py:29
  76.0 0.1 select_add_fusion
  76.1 0.1 fusion.17
  76.2 0.7 copy-done.3
  76.9 6.3 %psum.16 = f32[8,128]{1,0:T(8,128)} all-reduce(f32[8,128]{1,0:T(8,128)S(1)} %add.377), channel_id=1, replica_groups=mesh['lon'=8,'bin'=4] {'bin'}, use_global_device_ids=true, to_apply=%region_1.2 | all-reduce | flops 1024 | bytes 8192 | tf_op jit(solution)/shard_map/psum | solution.py:146
  (64 shorter events, 0.8 us)
Async XLA Ops:
  0.6 0.8 copy-start
  1.4 0.8 copy-start.2
  2.3 6.0 %copy-start.4 = (f32[4,8]{1,0:T(4,128)S(1)}, f32[4,8]{1,0:T(4,128)}, u32[]{:S(2)}) copy-start(f32[4,8]{1,0:T(4,128)} %param.10) | copy-start | bytes 388
  2.3 7.6 %collective-permute-start = (f32[2,4,8,3]{3,2,1,0:T(8,128)S(1)}, f32[2,4,8,3]{3,2,1,0:T(8,128)S(1)}, u32[]{:S(2)}, u32[]{:S(2)}) collective-permute-start(f32[2,4,8,3]{3,2,1,0:T(8,128)S(1)} %get-tuple-element.30), channel_id=1, source_target_pairs={{4,0},{8,4},{12,8},{16,12},{20,16},{24,20},{28,24},{0,28},{5,1},{9... | collective-permute-start | bytes 2312 | tf_op jit(solution)/shard_map/ppermute | solution.py:22
  8.3 0.7 copy-start.5
  8.3 6.6 %collective-permute-start.1 = (f32[2,4,8,3]{3,2,1,0:T(8,128)S(1)}, f32[2,4,8,3]{3,2,1,0:T(8,128)S(1)}, u32[]{:S(2)}, u32[]{:S(2)}) collective-permute-start(f32[2,4,8,3]{3,2,1,0:T(8,128)S(1)} %get-tuple-element.31), channel_id=1, source_target_pairs={{0,4},{4,8},{8,12},{12,16},{16,20},{20,24},{24,28},{28,0},{1,5},{5... | collective-permute-start | bytes 2312 | tf_op jit(solution)/shard_map/ppermute | solution.py:19
  15.2 0.7 copy-start.6
  15.3 3.9 %collective-permute-start.2 = (f32[2,4,8,128]{3,2,1,0:T(8,128)S(1)}, f32[2,4,8,128]{3,2,1,0:T(8,128)S(1)}, u32[]{:S(2)}, u32[]{:S(2)}) collective-permute-start(f32[2,4,8,128]{3,2,1,0:T(8,128)S(1)} %slice_add_fusion.3), channel_id=1, source_target_pairs={{0,28},{4,0},{8,4},{12,8},{16,12},{20,16},{24,20},{28,24},{1,29},{... | collective-permute-start | bytes 98312 | tf_op jit(solution)/shard_map/ppermute | solution.py:29
  20.6 18.2 %copy-start.7 = (f32[4]{0:T(128)S(1)}, f32[4]{0:T(128)}, u32[]{:S(2)}) copy-start(f32[4]{0:T(128)} %param.11) | copy-start | bytes 52
  20.6 6.6 %collective-permute-start.4 = (f32[2,4,8,128]{3,2,1,0:T(8,128)S(1)}, f32[2,4,8,128]{3,2,1,0:T(8,128)S(1)}, u32[]{:S(2)}, u32[]{:S(2)}) collective-permute-start(f32[2,4,8,128]{3,2,1,0:T(8,128)S(1)} %broadcast_select_fusion.1), channel_id=1, source_target_pairs={{0,4},{4,8},{8,12},{12,16},{16,20},{20,24},{24,28},{28,0},{1,5},{5... | collective-permute-start | bytes 98312 | tf_op jit(solution)/shard_map/ppermute | solution.py:29
  20.6 6.6 %collective-permute-start.3 = (f32[2,4,8,128]{3,2,1,0:T(8,128)S(1)}, f32[2,4,8,128]{3,2,1,0:T(8,128)S(1)}, u32[]{:S(2)}, u32[]{:S(2)}) collective-permute-start(f32[2,4,8,128]{3,2,1,0:T(8,128)S(1)} %get-tuple-element.10), channel_id=1, source_target_pairs={{0,28},{4,0},{8,4},{12,8},{16,12},{20,16},{24,20},{28,24},{1,29},{... | collective-permute-start | bytes 98312 | tf_op jit(solution)/shard_map/ppermute | solution.py:29
  27.2 6.6 %collective-permute-start.6 = (f32[2,4,8,128]{3,2,1,0:T(8,128)S(1)}, f32[2,4,8,128]{3,2,1,0:T(8,128)S(1)}, u32[]{:S(2)}, u32[]{:S(2)}) collective-permute-start(f32[2,4,8,128]{3,2,1,0:T(8,128)S(1)} %collective-permute-done.4), channel_id=1, source_target_pairs={{0,4},{4,8},{8,12},{12,16},{16,20},{20,24},{24,28},{28,0},{1,5},{5... | collective-permute-start | bytes 98312 | tf_op jit(solution)/shard_map/ppermute | solution.py:29
  27.2 6.6 %collective-permute-start.5 = (f32[2,4,8,128]{3,2,1,0:T(8,128)S(1)}, f32[2,4,8,128]{3,2,1,0:T(8,128)S(1)}, u32[]{:S(2)}, u32[]{:S(2)}) collective-permute-start(f32[2,4,8,128]{3,2,1,0:T(8,128)S(1)} %collective-permute-done.3), channel_id=1, source_target_pairs={{0,28},{4,0},{8,4},{12,8},{16,12},{20,16},{24,20},{28,24},{1,29},{... | collective-permute-start | bytes 98312 | tf_op jit(solution)/shard_map/ppermute | solution.py:29
  33.9 6.9 %collective-permute-start.8 = (f32[2,4,8,128]{3,2,1,0:T(8,128)S(1)}, f32[2,4,8,128]{3,2,1,0:T(8,128)S(1)}, u32[]{:S(2)}, u32[]{:S(2)}) collective-permute-start(f32[2,4,8,128]{3,2,1,0:T(8,128)S(1)} %collective-permute-done.6), channel_id=1, source_target_pairs={{0,4},{4,8},{8,12},{12,16},{16,20},{20,24},{24,28},{28,0},{1,5},{5... | collective-permute-start | bytes 98312 | tf_op jit(solution)/shard_map/ppermute | solution.py:29
  33.9 6.9 %collective-permute-start.7 = (f32[2,4,8,128]{3,2,1,0:T(8,128)S(1)}, f32[2,4,8,128]{3,2,1,0:T(8,128)S(1)}, u32[]{:S(2)}, u32[]{:S(2)}) collective-permute-start(f32[2,4,8,128]{3,2,1,0:T(8,128)S(1)} %collective-permute-done.5), channel_id=1, source_target_pairs={{0,28},{4,0},{8,4},{12,8},{16,12},{20,16},{24,20},{28,24},{1,29},{... | collective-permute-start | bytes 98312 | tf_op jit(solution)/shard_map/ppermute | solution.py:29
  41.1 6.6 %collective-permute-start.10 = (f32[2,4,8,3]{3,2,1,0:T(8,128)S(1)}, f32[2,4,8,3]{3,2,1,0:T(8,128)S(1)}, u32[]{:S(2)}, u32[]{:S(2)}) collective-permute-start(f32[2,4,8,3]{3,2,1,0:T(8,128)S(1)} %get-tuple-element.27), channel_id=1, source_target_pairs={{0,4},{4,8},{8,12},{12,16},{16,20},{20,24},{24,28},{28,0},{1,5},{5... | collective-permute-start | bytes 2312 | tf_op jit(solution)/shard_map/ppermute | solution.py:19
  41.1 6.6 %collective-permute-start.9 = (f32[2,4,8,3]{3,2,1,0:T(8,128)S(1)}, f32[2,4,8,3]{3,2,1,0:T(8,128)S(1)}, u32[]{:S(2)}, u32[]{:S(2)}) collective-permute-start(f32[2,4,8,3]{3,2,1,0:T(8,128)S(1)} %get-tuple-element.26), channel_id=1, source_target_pairs={{4,0},{8,4},{12,8},{16,12},{20,16},{24,20},{28,24},{0,28},{5,1},{9... | collective-permute-start | bytes 2312 | tf_op jit(solution)/shard_map/ppermute | solution.py:22
  48.1 6.3 %collective-permute-start.11 = (f32[2,4,8,128]{3,2,1,0:T(8,128)S(1)}, f32[2,4,8,128]{3,2,1,0:T(8,128)S(1)}, u32[]{:S(2)}, u32[]{:S(2)}) collective-permute-start(f32[2,4,8,128]{3,2,1,0:T(8,128)S(1)} %slice_add_fusion.1), channel_id=1, source_target_pairs={{0,28},{4,0},{8,4},{12,8},{16,12},{20,16},{24,20},{28,24},{1,29},{... | collective-permute-start | bytes 98312 | tf_op jit(solution)/shard_map/ppermute | solution.py:29
  55.9 6.9 %collective-permute-start.13 = (f32[2,4,8,128]{3,2,1,0:T(8,128)S(1)}, f32[2,4,8,128]{3,2,1,0:T(8,128)S(1)}, u32[]{:S(2)}, u32[]{:S(2)}) collective-permute-start(f32[2,4,8,128]{3,2,1,0:T(8,128)S(1)} %broadcast_select_fusion), channel_id=1, source_target_pairs={{0,4},{4,8},{8,12},{12,16},{16,20},{20,24},{24,28},{28,0},{1,5},{5... | collective-permute-start | bytes 98312 | tf_op jit(solution)/shard_map/ppermute | solution.py:29
  55.9 6.9 %collective-permute-start.12 = (f32[2,4,8,128]{3,2,1,0:T(8,128)S(1)}, f32[2,4,8,128]{3,2,1,0:T(8,128)S(1)}, u32[]{:S(2)}, u32[]{:S(2)}) collective-permute-start(f32[2,4,8,128]{3,2,1,0:T(8,128)S(1)} %get-tuple-element.4), channel_id=1, source_target_pairs={{0,28},{4,0},{8,4},{12,8},{16,12},{20,16},{24,20},{28,24},{1,29},{... | collective-permute-start | bytes 98312 | tf_op jit(solution)/shard_map/ppermute | solution.py:29
  62.8 6.6 %collective-permute-start.15 = (f32[2,4,8,128]{3,2,1,0:T(8,128)S(1)}, f32[2,4,8,128]{3,2,1,0:T(8,128)S(1)}, u32[]{:S(2)}, u32[]{:S(2)}) collective-permute-start(f32[2,4,8,128]{3,2,1,0:T(8,128)S(1)} %collective-permute-done.13), channel_id=1, source_target_pairs={{0,4},{4,8},{8,12},{12,16},{16,20},{20,24},{24,28},{28,0},{1,5},{5... | collective-permute-start | bytes 98312 | tf_op jit(solution)/shard_map/ppermute | solution.py:29
  62.8 6.6 %collective-permute-start.14 = (f32[2,4,8,128]{3,2,1,0:T(8,128)S(1)}, f32[2,4,8,128]{3,2,1,0:T(8,128)S(1)}, u32[]{:S(2)}, u32[]{:S(2)}) collective-permute-start(f32[2,4,8,128]{3,2,1,0:T(8,128)S(1)} %collective-permute-done.12), channel_id=1, source_target_pairs={{0,28},{4,0},{8,4},{12,8},{16,12},{20,16},{24,20},{28,24},{1,29},{... | collective-permute-start | bytes 98312 | tf_op jit(solution)/shard_map/ppermute | solution.py:29
  69.4 6.6 %collective-permute-start.17 = (f32[2,4,8,128]{3,2,1,0:T(8,128)S(1)}, f32[2,4,8,128]{3,2,1,0:T(8,128)S(1)}, u32[]{:S(2)}, u32[]{:S(2)}) collective-permute-start(f32[2,4,8,128]{3,2,1,0:T(8,128)S(1)} %collective-permute-done.15), channel_id=1, source_target_pairs={{0,4},{4,8},{8,12},{12,16},{16,20},{20,24},{24,28},{28,0},{1,5},{5... | collective-permute-start | bytes 98312 | tf_op jit(solution)/shard_map/ppermute | solution.py:29
  69.4 6.6 %collective-permute-start.16 = (f32[2,4,8,128]{3,2,1,0:T(8,128)S(1)}, f32[2,4,8,128]{3,2,1,0:T(8,128)S(1)}, u32[]{:S(2)}, u32[]{:S(2)}) collective-permute-start(f32[2,4,8,128]{3,2,1,0:T(8,128)S(1)} %collective-permute-done.14), channel_id=1, source_target_pairs={{0,28},{4,0},{8,4},{12,8},{16,12},{20,16},{24,20},{28,24},{1,29},{... | collective-permute-start | bytes 98312 | tf_op jit(solution)/shard_map/ppermute | solution.py:29
  76.2 0.7 copy-start.3
  76.9 6.3 %copy-start.1 = (f32[2,4,8,128]{3,2,1,0:T(8,128)}, f32[2,4,8,128]{3,2,1,0:T(8,128)S(1)}, u32[]{:S(2)}) copy-start(f32[2,4,8,128]{3,2,1,0:T(8,128)S(1)} %slice_add_fusion) | copy-start | bytes 98308
where the time goes:
time: 83.5 us; the launch traced here: 83.2 us
  starting transfers between devices  44.6 us (53%)
  waiting for transfers between devices  23.9 us (29%)
  blocking collectives  6.26 us (7%)
  local copies, waits for them, and re-layouts  3.77 us (5%)
  other arithmetic  3.62 us (4%)
  between operations  1.04 us (1%)
    ppermute x14, starting transfers between devices, from_behind(): lax.ppermute(value, axis, [(i, (i + by) % length) for i in range(length)])  33.8 us
    ppermute x14, waiting for transfers between devices, from_behind(): lax.ppermute(value, axis, [(i, (i + by) % length) for i in range(length)])  16.1 us
    ppermute x2, starting transfers between devices, padded_2(): lax.ppermute(lax.slice_in_dim(block, 0, width, axis=dim), axis, backward)  10.7 us
    ppermute x2, waiting for transfers between devices, padded_2(): lax.ppermute(lax.slice_in_dim(block, block.shape[dim] - width, None, axis...  6.9 us
    psum x1, blocking collectives, per_device(): gradient_sum = gradient_sum + lax.psum(local_term, 'bin')  6.26 us
    unnamed x16, local copies, waits for them, and re-layouts  2.61 us
  transfers between devices with their start and end apart: 18, of which 11 were waited for; matrix products, arithmetic and copies ran while one was open for 0% of the time, Pallas kernels for 0%

commit v1 on v0

--- a/solution.py
+++ b/solution.py
@@ -2,12 +2,17 @@
 import jax.numpy as jnp
 from jax import lax
 from jax.sharding import PartitionSpec as P
+from jax.lax import all_gather
 
 HMAX = 3
 STEPS = 2
 right_face = (0.0, -1.0, 7.0, 7.0, -1.0)
 slope_face = (1.0, -8.0, 0.0, 8.0, -1.0)
 curve_face = (3.0, -18.0, 30.0, -18.0, 3.0)
+
+
+def set_panel_on_mesh(raw, axis_name):
+    return jnp.sum(all_gather(raw, axis_name), 0)
 
 
 def padded_2(block, sides, width):
@@ -143,7 +148,7 @@
         adjoint_field = hop_shift(adjoint_field, zonal_hops, cell_shift)
         adjoint_field = meridional_adjoint(adjoint_field, meridional_fraction)
         local_term = jnp.sum(base_flux * adjoint_field[:, 0], axis=0)
-        gradient_sum = gradient_sum + lax.psum(local_term, "bin")
+        gradient_sum = gradient_sum + set_panel_on_mesh(local_term, "bin")
     return (adjoint_field, gradient_sum)
 
 

time: 83.5 us -> 88.2 us (1.056)
  blocking collectives: 6.26 us -> 10.4 us
    all_gather x0 -> x2, blocking collectives: none -> 10.4 us  [set_panel_on_mesh(): return jnp.sum(all_gather(raw, axis_name), 0)]
    psum x1 -> x0, blocking collectives: 6.26 us -> none  [per_device(): gradient_sum = gradient_sum + lax.psum(local_term, 'bin')]
where the time goes in v1:
time: 88.2 us; the launch traced here: 87.9 us
  starting transfers between devices  44.6 us (51%)
  waiting for transfers between devices  23.9 us (27%)
  blocking collectives  10.4 us (12%)
  other arithmetic  4.22 us (5%)
  local copies, waits for them, and re-layouts  3.77 us (4%)
  between operations  1.04 us (1%)
    ppermute x14, starting transfers between devices, from_behind(): lax.ppermute(value, axis, [(i, (i + by) % length) for i in range(length)])  33.8 us
    ppermute x14, waiting for transfers between devices, from_behind(): lax.ppermute(value, axis, [(i, (i + by) % length) for i in range(length)])  16.1 us
    ppermute x2, starting transfers between devices, padded_2(): lax.ppermute(lax.slice_in_dim(block, 0, width, axis=dim), axis, backward)  10.7 us
    all_gather x2, blocking collectives, set_panel_on_mesh(): return jnp.sum(all_gather(raw, axis_name), 0)  10.4 us
    ppermute x2, waiting for transfers between devices, padded_2(): lax.ppermute(lax.slice_in_dim(block, block.shape[dim] - width, None, axis...  6.9 us
    unnamed x16, local copies, waits for them, and re-layouts  2.61 us
  transfers between devices with their start and end apart: 18, of which 11 were waited for; matrix products, arithmetic and copies ran while one was open for 0% of the time, Pallas kernels for 0%

profile of v1, /device:TPU:0, one launch (start us, length us, event | category | flops | bytes accessed | tf_op | source)
XLA Modules:
  0.0 87.9 jit_solution(13490388088320036954)
XLA Ops:
  0.6 0.8 fusion.54
  1.4 0.7 copy-done.2
  2.3 6.0 %collective-permute-start = (f32[2,4,8,3]{3,2,1,0:T(8,128)S(1)}, f32[2,4,8,3]{3,2,1,0:T(8,128)S(1)}, u32[]{:S(2)}, u32[]{:S(2)}) collective-permute-start(f32[2,4,8,3]{3,2,1,0:T(8,128)S(1)} %get-tuple-element.30), channel_id=1, source_target_pairs={{4,0},{8,4},{12,8},{16,12},{20,16},{24,20},{28,24},{0,28},{5,1},{9... | collective-permute-start | bytes 2312 | tf_op jit(solution)/shard_map/ppermute | solution.py:27
  8.3 0.6 copy-done.5
  9.0 0.9 %collective-permute-done = f32[2,4,8,3]{3,2,1,0:T(8,128)S(1)} collective-permute-done((f32[2,4,8,3]{3,2,1,0:T(8,128)S(1)}, f32[2,4,8,3]{3,2,1,0:T(8,128)S(1)}, u32[]{:S(2)}, u32[]{:S(2)}) %collective-permute-start) | collective-permute-done | bytes 800 | tf_op jit(solution)/shard_map/ppermute | solution.py:27
  9.9 5.0 %collective-permute-done.1 = f32[2,4,8,3]{3,2,1,0:T(8,128)S(1)} collective-permute-done((f32[2,4,8,3]{3,2,1,0:T(8,128)S(1)}, f32[2,4,8,3]{3,2,1,0:T(8,128)S(1)}, u32[]{:S(2)}, u32[]{:S(2)}) %collective-permute-start.1) | collective-permute-done | bytes 800 | tf_op jit(solution)/shard_map/ppermute | solution.py:24
  14.9 0.1 pad_maximum_fusion.2
  15.0 0.2 fusion.26
  15.2 0.1 slice_add_fusion.3
  15.3 0.6 copy-done.6
  15.9 3.3 %collective-permute-done.2 = f32[2,4,8,128]{3,2,1,0:T(8,128)S(1)} collective-permute-done((f32[2,4,8,128]{3,2,1,0:T(8,128)S(1)}, f32[2,4,8,128]{3,2,1,0:T(8,128)S(1)}, u32[]{:S(2)}, u32[]{:S(2)}) %collective-permute-start.2) | collective-permute-done | bytes 32800 | tf_op jit(solution)/shard_map/ppermute | solution.py:34
  19.2 0.1 fusion.2
  19.3 0.1 fusion.3
  19.4 0.1 slice.368
  19.5 0.1 maximum_select_fusion
  19.5 0.1 slice.370
  19.6 0.1 maximum_select_fusion.1
  19.7 0.1 slice.372
  19.8 0.1 maximum_select_fusion.2
  19.9 0.1 slice.374
  20.0 0.1 maximum_select_fusion.3
  20.1 0.1 slice.376
  20.2 0.1 maximum_select_fusion.4
  20.3 0.1 slice.378
  20.4 0.1 maximum_select_fusion.5
  20.5 0.1 broadcast_select_fusion.2
  20.6 4.7 %collective-permute-start.3 = (f32[2,4,8,128]{3,2,1,0:T(8,128)S(1)}, f32[2,4,8,128]{3,2,1,0:T(8,128)S(1)}, u32[]{:S(2)}, u32[]{:S(2)}) collective-permute-start(f32[2,4,8,128]{3,2,1,0:T(8,128)S(1)} %get-tuple-element.10), channel_id=1, source_target_pairs={{0,28},{4,0},{8,4},{12,8},{16,12},{20,16},{24,20},{28,24},{1,29},{... | collective-permute-start | bytes 98312 | tf_op jit(solution)/shard_map/ppermute | solution.py:34
  25.4 1.9 %collective-permute-done.4 = f32[2,4,8,128]{3,2,1,0:T(8,128)S(1)} collective-permute-done((f32[2,4,8,128]{3,2,1,0:T(8,128)S(1)}, f32[2,4,8,128]{3,2,1,0:T(8,128)S(1)}, u32[]{:S(2)}, u32[]{:S(2)}) %collective-permute-start.4) | collective-permute-done | bytes 32800 | tf_op jit(solution)/shard_map/ppermute | solution.py:34
  27.2 4.8 %collective-permute-start.5 = (f32[2,4,8,128]{3,2,1,0:T(8,128)S(1)}, f32[2,4,8,128]{3,2,1,0:T(8,128)S(1)}, u32[]{:S(2)}, u32[]{:S(2)}) collective-permute-start(f32[2,4,8,128]{3,2,1,0:T(8,128)S(1)} %collective-permute-done.3), channel_id=1, source_target_pairs={{0,28},{4,0},{8,4},{12,8},{16,12},{20,16},{24,20},{28,24},{1,29},{... | collective-permute-start | bytes 98312 | tf_op jit(solution)/shard_map/ppermute | solution.py:34
  32.1 1.8 %collective-permute-done.6 = f32[2,4,8,128]{3,2,1,0:T(8,128)S(1)} collective-permute-done((f32[2,4,8,128]{3,2,1,0:T(8,128)S(1)}, f32[2,4,8,128]{3,2,1,0:T(8,128)S(1)}, u32[]{:S(2)}, u32[]{:S(2)}) %collective-permute-start.6) | collective-permute-done | bytes 32800 | tf_op jit(solution)/shard_map/ppermute | solution.py:34
  33.9 5.0 %collective-permute-start.7 = (f32[2,4,8,128]{3,2,1,0:T(8,128)S(1)}, f32[2,4,8,128]{3,2,1,0:T(8,128)S(1)}, u32[]{:S(2)}, u32[]{:S(2)}) collective-permute-start(f32[2,4,8,128]{3,2,1,0:T(8,128)S(1)} %collective-permute-done.5), channel_id=1, source_target_pairs={{0,28},{4,0},{8,4},{12,8},{16,12},{20,16},{24,20},{28,24},{1,29},{... | collective-permute-start | bytes 98312 | tf_op jit(solution)/shard_map/ppermute | solution.py:34
  38.8 2.0 %collective-permute-done.8 = f32[2,4,8,128]{3,2,1,0:T(8,128)S(1)} collective-permute-done((f32[2,4,8,128]{3,2,1,0:T(8,128)S(1)}, f32[2,4,8,128]{3,2,1,0:T(8,128)S(1)}, u32[]{:S(2)}, u32[]{:S(2)}) %collective-permute-start.8) | collective-permute-done | bytes 32800 | tf_op jit(solution)/shard_map/ppermute | solution.py:34
  40.8 0.1 select_add_fusion.1
  40.9 0.1 fusion.8
  41.1 4.7 %collective-permute-start.9 = (f32[2,4,8,3]{3,2,1,0:T(8,128)S(1)}, f32[2,4,8,3]{3,2,1,0:T(8,128)S(1)}, u32[]{:S(2)}, u32[]{:S(2)}) collective-permute-start(f32[2,4,8,3]{3,2,1,0:T(8,128)S(1)} %get-tuple-element.26), channel_id=1, source_target_pairs={{4,0},{8,4},{12,8},{16,12},{20,16},{24,20},{28,24},{0,28},{5,1},{9... | collective-permute-start | bytes 2312 | tf_op jit(solution)/shard_map/ppermute | solution.py:27
  45.9 1.9 %collective-permute-done.10 = f32[2,4,8,3]{3,2,1,0:T(8,128)S(1)} collective-permute-done((f32[2,4,8,3]{3,2,1,0:T(8,128)S(1)}, f32[2,4,8,3]{3,2,1,0:T(8,128)S(1)}, u32[]{:S(2)}, u32[]{:S(2)}) %collective-permute-start.10) | collective-permute-done | bytes 800 | tf_op jit(solution)/shard_map/ppermute | solution.py:24
  47.8 0.1 pad_maximum_fusion.3
  47.8 0.2 fusion.22
  48.0 0.1 slice_add_fusion.1
  48.1 4.7 %collective-permute-start.11 = (f32[2,4,8,128]{3,2,1,0:T(8,128)S(1)}, f32[2,4,8,128]{3,2,1,0:T(8,128)S(1)}, u32[]{:S(2)}, u32[]{:S(2)}) collective-permute-start(f32[2,4,8,128]{3,2,1,0:T(8,128)S(1)} %slice_add_fusion.1), channel_id=1, source_target_pairs={{0,28},{4,0},{8,4},{12,8},{16,12},{20,16},{24,20},{28,24},{1,29},{... | collective-permute-start | bytes 98312 | tf_op jit(solution)/shard_map/ppermute | solution.py:34
  52.8 1.6 %collective-permute-done.11 = f32[2,4,8,128]{3,2,1,0:T(8,128)S(1)} collective-permute-done((f32[2,4,8,128]{3,2,1,0:T(8,128)S(1)}, f32[2,4,8,128]{3,2,1,0:T(8,128)S(1)}, u32[]{:S(2)}, u32[]{:S(2)}) %collective-permute-start.11) | collective-permute-done | bytes 32800 | tf_op jit(solution)/shard_map/ppermute | solution.py:34
  54.4 0.1 fusion
  54.5 0.1 fusion.1
  54.6 0.1 slice.401
  54.7 0.1 maximum_select_fusion.6
  54.9 0.1 maximum_select_fusion.7
  55.0 0.1 maximum_select_fusion.8
  55.1 0.1 slice.407
  55.2 0.1 maximum_select_fusion.9
  55.4 0.1 maximum_select_fusion.10
  55.6 0.1 maximum_select_fusion.11
  55.7 0.1 broadcast_select_fusion.3
  55.9 5.1 %collective-permute-start.12 = (f32[2,4,8,128]{3,2,1,0:T(8,128)S(1)}, f32[2,4,8,128]{3,2,1,0:T(8,128)S(1)}, u32[]{:S(2)}, u32[]{:S(2)}) collective-permute-start(f32[2,4,8,128]{3,2,1,0:T(8,128)S(1)} %get-tuple-element.4), channel_id=1, source_target_pairs={{0,28},{4,0},{8,4},{12,8},{16,12},{20,16},{24,20},{28,24},{1,29},{... | collective-permute-start | bytes 98312 | tf_op jit(solution)/shard_map/ppermute | solution.py:34
  60.9 1.8 %collective-permute-done.13 = f32[2,4,8,128]{3,2,1,0:T(8,128)S(1)} collective-permute-done((f32[2,4,8,128]{3,2,1,0:T(8,128)S(1)}, f32[2,4,8,128]{3,2,1,0:T(8,128)S(1)}, u32[]{:S(2)}, u32[]{:S(2)}) %collective-permute-start.13) | collective-permute-done | bytes 32800 | tf_op jit(solution)/shard_map/ppermute | solution.py:34
  62.8 4.8 %collective-permute-start.14 = (f32[2,4,8,128]{3,2,1,0:T(8,128)S(1)}, f32[2,4,8,128]{3,2,1,0:T(8,128)S(1)}, u32[]{:S(2)}, u32[]{:S(2)}) collective-permute-start(f32[2,4,8,128]{3,2,1,0:T(8,128)S(1)} %collective-permute-done.12), channel_id=1, source_target_pairs={{0,28},{4,0},{8,4},{12,8},{16,12},{20,16},{24,20},{28,24},{1,29},{... | collective-permute-start | bytes 98312 | tf_op jit(solution)/shard_map/ppermute | solution.py:34
  67.5 1.8 %collective-permute-done.15 = f32[2,4,8,128]{3,2,1,0:T(8,128)S(1)} collective-permute-done((f32[2,4,8,128]{3,2,1,0:T(8,128)S(1)}, f32[2,4,8,128]{3,2,1,0:T(8,128)S(1)}, u32[]{:S(2)}, u32[]{:S(2)}) %collective-permute-start.15) | collective-permute-done | bytes 32800 | tf_op jit(solution)/shard_map/ppermute | solution.py:34
  69.4 4.8 %collective-permute-start.16 = (f32[2,4,8,128]{3,2,1,0:T(8,128)S(1)}, f32[2,4,8,128]{3,2,1,0:T(8,128)S(1)}, u32[]{:S(2)}, u32[]{:S(2)}) collective-permute-start(f32[2,4,8,128]{3,2,1,0:T(8,128)S(1)} %collective-permute-done.14), channel_id=1, source_target_pairs={{0,28},{4,0},{8,4},{12,8},{16,12},{20,16},{24,20},{28,24},{1,29},{... | collective-permute-start | bytes 98312 | tf_op jit(solution)/shard_map/ppermute | solution.py:34
  74.2 1.8 %collective-permute-done.17 = f32[2,4,8,128]{3,2,1,0:T(8,128)S(1)} collective-permute-done((f32[2,4,8,128]{3,2,1,0:T(8,128)S(1)}, f32[2,4,8,128]{3,2,1,0:T(8,128)S(1)}, u32[]{:S(2)}, u32[]{:S(2)}) %collective-permute-start.17) | collective-permute-done | bytes 32800 | tf_op jit(solution)/shard_map/ppermute | solution.py:34
  76.0 0.1 select_add_fusion
  76.1 0.1 fusion.17
  76.2 0.7 copy-done.3
  76.9 5.2 %all-gather.1 = f32[32,128]{1,0:T(8,128)S(1)} all-gather(f32[8,128]{1,0:T(8,128)S(1)} %get-tuple-element.2), channel_id=3, replica_groups=mesh['lon'=8,'bin'=4] {'bin'}, dimensions={0}, use_global_device_ids=true | all-gather | bytes 20480 | tf_op jit(solution)/shard_map/all_gather | solution.py:15
  82.1 5.2 %all-gather = f32[32,128]{1,0:T(8,128)S(1)} all-gather(f32[8,128]{1,0:T(8,128)S(1)} %get-tuple-element.3), channel_id=2, replica_groups=mesh['lon'=8,'bin'=4] {'bin'}, dimensions={0}, use_global_device_ids=true | all-gather | bytes 20480 | tf_op jit(solution)/shard_map/all_gather | solution.py:15
  87.3 0.6 add.373
  (67 shorter events, 1.0 us)
Async XLA Ops:
  0.6 0.8 copy-start
  1.4 0.8 copy-start.2
  2.3 6.0 %copy-start.4 = (f32[4,8]{1,0:T(4,128)S(1)}, f32[4,8]{1,0:T(4,128)}, u32[]{:S(2)}) copy-start(f32[4,8]{1,0:T(4,128)} %param.10) | copy-start | bytes 388
  2.3 7.6 %collective-permute-start = (f32[2,4,8,3]{3,2,1,0:T(8,128)S(1)}, f32[2,4,8,3]{3,2,1,0:T(8,128)S(1)}, u32[]{:S(2)}, u32[]{:S(2)}) collective-permute-start(f32[2,4,8,3]{3,2,1,0:T(8,128)S(1)} %get-tuple-element.30), channel_id=1, source_target_pairs={{4,0},{8,4},{12,8},{16,12},{20,16},{24,20},{28,24},{0,28},{5,1},{9... | collective-permute-start | bytes 2312 | tf_op jit(solution)/shard_map/ppermute | solution.py:27
  8.3 0.7 copy-start.5
  8.3 6.6 %collective-permute-start.1 = (f32[2,4,8,3]{3,2,1,0:T(8,128)S(1)}, f32[2,4,8,3]{3,2,1,0:T(8,128)S(1)}, u32[]{:S(2)}, u32[]{:S(2)}) collective-permute-start(f32[2,4,8,3]{3,2,1,0:T(8,128)S(1)} %get-tuple-element.31), channel_id=1, source_target_pairs={{0,4},{4,8},{8,12},{12,16},{16,20},{20,24},{24,28},{28,0},{1,5},{5... | collective-permute-start | bytes 2312 | tf_op jit(solution)/shard_map/ppermute | solution.py:24
  15.2 0.7 copy-start.6
  15.3 3.9 %collective-permute-start.2 = (f32[2,4,8,128]{3,2,1,0:T(8,128)S(1)}, f32[2,4,8,128]{3,2,1,0:T(8,128)S(1)}, u32[]{:S(2)}, u32[]{:S(2)}) collective-permute-start(f32[2,4,8,128]{3,2,1,0:T(8,128)S(1)} %slice_add_fusion.3), channel_id=1, source_target_pairs={{0,28},{4,0},{8,4},{12,8},{16,12},{20,16},{24,20},{28,24},{1,29},{... | collective-permute-start | bytes 98312 | tf_op jit(solution)/shard_map/ppermute | solution.py:34
  20.6 18.2 %copy-start.7 = (f32[4]{0:T(128)S(1)}, f32[4]{0:T(128)}, u32[]{:S(2)}) copy-start(f32[4]{0:T(128)} %param.11) | copy-start | bytes 52
  20.6 6.6 %collective-permute-start.4 = (f32[2,4,8,128]{3,2,1,0:T(8,128)S(1)}, f32[2,4,8,128]{3,2,1,0:T(8,128)S(1)}, u32[]{:S(2)}, u32[]{:S(2)}) collective-permute-start(f32[2,4,8,128]{3,2,1,0:T(8,128)S(1)} %broadcast_select_fusion.1), channel_id=1, source_target_pairs={{0,4},{4,8},{8,12},{12,16},{16,20},{20,24},{24,28},{28,0},{1,5},{5... | collective-permute-start | bytes 98312 | tf_op jit(solution)/shard_map/ppermute | solution.py:34
  20.6 6.6 %collective-permute-start.3 = (f32[2,4,8,128]{3,2,1,0:T(8,128)S(1)}, f32[2,4,8,128]{3,2,1,0:T(8,128)S(1)}, u32[]{:S(2)}, u32[]{:S(2)}) collective-permute-start(f32[2,4,8,128]{3,2,1,0:T(8,128)S(1)} %get-tuple-element.10), channel_id=1, source_target_pairs={{0,28},{4,0},{8,4},{12,8},{16,12},{20,16},{24,20},{28,24},{1,29},{... | collective-permute-start | bytes 98312 | tf_op jit(solution)/shard_map/ppermute | solution.py:34
  27.2 6.6 %collective-permute-start.6 = (f32[2,4,8,128]{3,2,1,0:T(8,128)S(1)}, f32[2,4,8,128]{3,2,1,0:T(8,128)S(1)}, u32[]{:S(2)}, u32[]{:S(2)}) collective-permute-start(f32[2,4,8,128]{3,2,1,0:T(8,128)S(1)} %collective-permute-done.4), channel_id=1, source_target_pairs={{0,4},{4,8},{8,12},{12,16},{16,20},{20,24},{24,28},{28,0},{1,5},{5... | collective-permute-start | bytes 98312 | tf_op jit(solution)/shard_map/ppermute | solution.py:34
  27.2 6.6 %collective-permute-start.5 = (f32[2,4,8,128]{3,2,1,0:T(8,128)S(1)}, f32[2,4,8,128]{3,2,1,0:T(8,128)S(1)}, u32[]{:S(2)}, u32[]{:S(2)}) collective-permute-start(f32[2,4,8,128]{3,2,1,0:T(8,128)S(1)} %collective-permute-done.3), channel_id=1, source_target_pairs={{0,28},{4,0},{8,4},{12,8},{16,12},{20,16},{24,20},{28,24},{1,29},{... | collective-permute-start | bytes 98312 | tf_op jit(solution)/shard_map/ppermute | solution.py:34
  33.9 6.9 %collective-permute-start.8 = (f32[2,4,8,128]{3,2,1,0:T(8,128)S(1)}, f32[2,4,8,128]{3,2,1,0:T(8,128)S(1)}, u32[]{:S(2)}, u32[]{:S(2)}) collective-permute-start(f32[2,4,8,128]{3,2,1,0:T(8,128)S(1)} %collective-permute-done.6), channel_id=1, source_target_pairs={{0,4},{4,8},{8,12},{12,16},{16,20},{20,24},{24,28},{28,0},{1,5},{5... | collective-permute-start | bytes 98312 | tf_op jit(solution)/shard_map/ppermute | solution.py:34
  33.9 6.9 %collective-permute-start.7 = (f32[2,4,8,128]{3,2,1,0:T(8,128)S(1)}, f32[2,4,8,128]{3,2,1,0:T(8,128)S(1)}, u32[]{:S(2)}, u32[]{:S(2)}) collective-permute-start(f32[2,4,8,128]{3,2,1,0:T(8,128)S(1)} %collective-permute-done.5), channel_id=1, source_target_pairs={{0,28},{4,0},{8,4},{12,8},{16,12},{20,16},{24,20},{28,24},{1,29},{... | collective-permute-start | bytes 98312 | tf_op jit(solution)/shard_map/ppermute | solution.py:34
  41.1 6.6 %collective-permute-start.10 = (f32[2,4,8,3]{3,2,1,0:T(8,128)S(1)}, f32[2,4,8,3]{3,2,1,0:T(8,128)S(1)}, u32[]{:S(2)}, u32[]{:S(2)}) collective-permute-start(f32[2,4,8,3]{3,2,1,0:T(8,128)S(1)} %get-tuple-element.27), channel_id=1, source_target_pairs={{0,4},{4,8},{8,12},{12,16},{16,20},{20,24},{24,28},{28,0},{1,5},{5... | collective-permute-start | bytes 2312 | tf_op jit(solution)/shard_map/ppermute | solution.py:24
  41.1 6.6 %collective-permute-start.9 = (f32[2,4,8,3]{3,2,1,0:T(8,128)S(1)}, f32[2,4,8,3]{3,2,1,0:T(8,128)S(1)}, u32[]{:S(2)}, u32[]{:S(2)}) collective-permute-start(f32[2,4,8,3]{3,2,1,0:T(8,128)S(1)} %get-tuple-element.26), channel_id=1, source_target_pairs={{4,0},{8,4},{12,8},{16,12},{20,16},{24,20},{28,24},{0,28},{5,1},{9... | collective-permute-start | bytes 2312 | tf_op jit(solution)/shard_map/ppermute | solution.py:27
  48.1 6.3 %collective-permute-start.11 = (f32[2,4,8,128]{3,2,1,0:T(8,128)S(1)}, f32[2,4,8,128]{3,2,1,0:T(8,128)S(1)}, u32[]{:S(2)}, u32[]{:S(2)}) collective-permute-start(f32[2,4,8,128]{3,2,1,0:T(8,128)S(1)} %slice_add_fusion.1), channel_id=1, source_target_pairs={{0,28},{4,0},{8,4},{12,8},{16,12},{20,16},{24,20},{28,24},{1,29},{... | collective-permute-start | bytes 98312 | tf_op jit(solution)/shard_map/ppermute | solution.py:34
  55.9 6.9 %collective-permute-start.13 = (f32[2,4,8,128]{3,2,1,0:T(8,128)S(1)}, f32[2,4,8,128]{3,2,1,0:T(8,128)S(1)}, u32[]{:S(2)}, u32[]{:S(2)}) collective-permute-start(f32[2,4,8,128]{3,2,1,0:T(8,128)S(1)} %broadcast_select_fusion), channel_id=1, source_target_pairs={{0,4},{4,8},{8,12},{12,16},{16,20},{20,24},{24,28},{28,0},{1,5},{5... | collective-permute-start | bytes 98312 | tf_op jit(solution)/shard_map/ppermute | solution.py:34
  55.9 6.9 %collective-permute-start.12 = (f32[2,4,8,128]{3,2,1,0:T(8,128)S(1)}, f32[2,4,8,128]{3,2,1,0:T(8,128)S(1)}, u32[]{:S(2)}, u32[]{:S(2)}) collective-permute-start(f32[2,4,8,128]{3,2,1,0:T(8,128)S(1)} %get-tuple-element.4), channel_id=1, source_target_pairs={{0,28},{4,0},{8,4},{12,8},{16,12},{20,16},{24,20},{28,24},{1,29},{... | collective-permute-start | bytes 98312 | tf_op jit(solution)/shard_map/ppermute | solution.py:34
  62.8 6.6 %collective-permute-start.15 = (f32[2,4,8,128]{3,2,1,0:T(8,128)S(1)}, f32[2,4,8,128]{3,2,1,0:T(8,128)S(1)}, u32[]{:S(2)}, u32[]{:S(2)}) collective-permute-start(f32[2,4,8,128]{3,2,1,0:T(8,128)S(1)} %collective-permute-done.13), channel_id=1, source_target_pairs={{0,4},{4,8},{8,12},{12,16},{16,20},{20,24},{24,28},{28,0},{1,5},{5... | collective-permute-start | bytes 98312 | tf_op jit(solution)/shard_map/ppermute | solution.py:34
  62.8 6.6 %collective-permute-start.14 = (f32[2,4,8,128]{3,2,1,0:T(8,128)S(1)}, f32[2,4,8,128]{3,2,1,0:T(8,128)S(1)}, u32[]{:S(2)}, u32[]{:S(2)}) collective-permute-start(f32[2,4,8,128]{3,2,1,0:T(8,128)S(1)} %collective-permute-done.12), channel_id=1, source_target_pairs={{0,28},{4,0},{8,4},{12,8},{16,12},{20,16},{24,20},{28,24},{1,29},{... | collective-permute-start | bytes 98312 | tf_op jit(solution)/shard_map/ppermute | solution.py:34
  69.4 6.6 %collective-permute-start.17 = (f32[2,4,8,128]{3,2,1,0:T(8,128)S(1)}, f32[2,4,8,128]{3,2,1,0:T(8,128)S(1)}, u32[]{:S(2)}, u32[]{:S(2)}) collective-permute-start(f32[2,4,8,128]{3,2,1,0:T(8,128)S(1)} %collective-permute-done.15), channel_id=1, source_target_pairs={{0,4},{4,8},{8,12},{12,16},{16,20},{20,24},{24,28},{28,0},{1,5},{5... | collective-permute-start | bytes 98312 | tf_op jit(solution)/shard_map/ppermute | solution.py:34
  69.4 6.6 %collective-permute-start.16 = (f32[2,4,8,128]{3,2,1,0:T(8,128)S(1)}, f32[2,4,8,128]{3,2,1,0:T(8,128)S(1)}, u32[]{:S(2)}, u32[]{:S(2)}) collective-permute-start(f32[2,4,8,128]{3,2,1,0:T(8,128)S(1)} %collective-permute-done.14), channel_id=1, source_target_pairs={{0,28},{4,0},{8,4},{12,8},{16,12},{20,16},{24,20},{28,24},{1,29},{... | collective-permute-start | bytes 98312 | tf_op jit(solution)/shard_map/ppermute | solution.py:34
  76.2 0.7 copy-start.3
  76.9 5.2 %copy-start.1 = (f32[2,4,8,128]{3,2,1,0:T(8,128)}, f32[2,4,8,128]{3,2,1,0:T(8,128)S(1)}, u32[]{:S(2)}) copy-start(f32[2,4,8,128]{3,2,1,0:T(8,128)S(1)} %slice_add_fusion) | copy-start | bytes 98308
